TPU v7x, 128 devices: a whole 4x4x4 slice. The times are simulated.
128 devices in a mesh: row: 8 (over z, core), col: 16 (over y, x).
Axes of the slice: x: 4, y: 4, z: 4, core: 2. Of those that a mesh axis runs over, the one named last changes fastest.
Arguments:
- children: bfloat16 [16384, 8192], P('row', 'col'), as said below
- child_maps: int32 [2, 64], replicated, may hold values from 0 to 127, as said below
- pattern: int32 [128, 128], replicated, may hold values from 0 to 1, as said below
- own_cols: bfloat16 [16384, 1024], P('row'), as said below
Outputs:
- updated_front: bfloat16 [16384, 16384], P('row', 'col')
- factor: float32 [16384, 1024], P(('row', 'col'))
Inputs may be any that keep to these rules, and one draw needn't show every extreme that they name: Each row of child_maps is injective. For each child and each a, of the 16 entries with indices a * 16 to (a + 1) * 16 - 1, exactly 2 lie in each range p * 16 to (p + 1) * 16 - 1. For each b, the 4 entries with indices b * 4 to (b + 1) * 4 - 1 lie in different ranges q * 8 to (q + 1) * 8 - 1. `pattern`: Symmetric; 1 on the diagonal, in every tile whose two indices are both below 8, and in every tile whose two indices are both in one child's map. `children`: each child's 8192 x 8192 block is symmetric. `own_cols`: rows 0 to 1023 form a symmetric matrix whose off-diagonal entries lie in [-3, 3] and whose diagonal entries lie between 4.5 * sqrt(1024) and 6.75 * sqrt(1024); added to the children's entries assembled there, it is positive definite.
All inputs are finite; a program needn't handle non-finite values.
Results may differ from a plain program's by a relative error of at most 0.001.
Values may be sent and summed in bfloat16 or wider, within the bound.
No kernel may reach another device: no remote copies, remote signals or barrier semaphores. Data moves between devices by JAX's collectives and lax.ppermute only.
A program may use at most 128 MiB of HBM per device.

v0:
```python
import jax
import jax.numpy as jnp
from jax import lax
from jax.sharding import PartitionSpec as P

BLK = 128
RB = 16
PW = 512
PANELS = 2


def broadcast(value, axis, source):
    kept = jnp.where(lax.axis_index(axis) == source, value, 0).astype(value.dtype)
    return lax.psum(kept, axis)


def body(children, child_maps, pattern, own_cols):
    row_count = lax.axis_size("row")
    col_count = lax.axis_size("col")
    row_index = lax.axis_index("row")
    col_index = lax.axis_index("col")
    half_rows = row_count // 2
    tile_size = BLK
    row_blocks = RB
    col_blocks = row_blocks // 2
    child_cols = row_blocks // 4
    slot_count = row_blocks // row_count
    group_maps = child_maps.reshape(row_count, row_blocks)
    column_maps = child_maps.reshape(2, col_count, child_cols)
    own_child = row_index // half_rows
    mine_rows = lax.dynamic_index_in_dim(group_maps, row_index, 0, keepdims=False)
    row_order = jnp.argsort(mine_rows // row_blocks, stable=True)
    child_tiles = children.reshape(row_blocks, tile_size, child_cols, tile_size)[row_order]
    child_tiles = child_tiles.reshape(row_count, slot_count, tile_size, child_cols, tile_size)
    targets = jnp.arange(col_count, dtype=jnp.int32)
    column_owner = column_maps // col_blocks
    column_hits = column_owner[:, :, None, :] == targets[None, None, :, None]
    selectors = column_hits.astype(jnp.bfloat16)
    direct_select = selectors[own_child][col_index]
    outgoing = jnp.einsum(
        "rkenf,pn->rpkef", child_tiles, direct_select, preferred_element_type=jnp.float32
    ).astype(jnp.bfloat16)
    outgoing = outgoing.reshape(row_count * col_count, slot_count, tile_size, tile_size)
    received = lax.all_to_all(outgoing, ("row", "col"), split_axis=0, concat_axis=0, tiled=True)
    other_rows = (group_maps // row_blocks != row_index).astype(jnp.int32)
    chosen = jnp.argsort(other_rows, axis=1, stable=True)[:, :slot_count]
    local_row = jnp.take_along_axis(group_maps, chosen, axis=1) % row_blocks
    owned_cols = column_owner == col_index
    has_col = jnp.repeat(jnp.any(owned_cols, axis=2), half_rows, axis=0)
    local_col = jnp.repeat(
        jnp.sum(jnp.where(owned_cols, column_maps % col_blocks, 0), axis=2), half_rows, axis=0
    )
    segment = local_row[:, None, :] * col_blocks + local_col[:, :, None]
    segment = jnp.where(has_col[:, :, None], segment, row_blocks * col_blocks)
    summed = jax.ops.segment_sum(
        received.astype(jnp.float32).reshape(-1, tile_size, tile_size),
        segment.reshape(-1),
        num_segments=row_blocks * col_blocks + 1,
    )
    front_matrix = summed[:-1].reshape(row_blocks, col_blocks, tile_size, tile_size)
    front_matrix = front_matrix.transpose(0, 2, 1, 3).reshape(
        row_blocks * tile_size, col_blocks * tile_size
    )
    own_part = jnp.where(col_index == 0, own_cols.astype(jnp.float32), 0.0)
    front_matrix = front_matrix.at[:, : PANELS * PW].add(own_part)
    block_pattern = lax.dynamic_slice(
        pattern, (row_index * row_blocks, col_index * col_blocks), (row_blocks, col_blocks)
    )
    tile_mask = block_pattern.astype(jnp.float32)
    front_matrix = (
        front_matrix.reshape(row_blocks, tile_size, col_blocks, tile_size)
        * tile_mask[:, None, :, None]
    ).reshape(row_blocks * tile_size, col_blocks * tile_size)
    global_rows = row_index * row_blocks * tile_size + jnp.arange(row_blocks * tile_size)
    row_block_ids = row_index * row_blocks + jnp.arange(row_blocks)
    col_block_ids = col_index * col_blocks + jnp.arange(col_blocks)
    share_rows = row_blocks * tile_size // col_count
    identity = jnp.eye(PW, dtype=jnp.float32)
    pieces = []
    for panel_index in range(PANELS):
        first_col = panel_index * PW
        strip_cols = broadcast(front_matrix[:, first_col : first_col + PW], "col", 0)
        diag_block = broadcast(strip_cols[first_col : first_col + PW], "row", 0)
        lower_factor = jnp.linalg.cholesky(diag_block)
        inverse = lax.linalg.triangular_solve(lower_factor, identity, left_side=True, lower=True)
        factor = jnp.dot(
            strip_cols,
            inverse.T,
            precision=lax.Precision.HIGHEST,
            preferred_element_type=jnp.float32,
        )
        factor = jnp.where(global_rows[:, None] >= first_col, factor, 0.0)
        pieces.append(lax.dynamic_slice_in_dim(factor, col_index * share_rows, share_rows, 0))
        own_rows = lax.dynamic_slice_in_dim(
            factor, col_index % 2 * col_blocks * tile_size, col_blocks * tile_size, 0
        )
        across = broadcast(own_rows, "row", col_index // 2)
        update = jnp.dot(
            factor, across.T, precision=lax.Precision.HIGHEST, preferred_element_type=jnp.float32
        )
        first_block = (first_col + PW) // tile_size
        keep_tiles = (
            tile_mask
            * (row_block_ids >= first_block)[:, None]
            * (col_block_ids >= first_block)[None, :]
        )
        front_matrix = front_matrix - (
            update.reshape(row_blocks, tile_size, col_blocks, tile_size)
            * keep_tiles[:, None, :, None]
        ).reshape(row_blocks * tile_size, col_blocks * tile_size)
    return (front_matrix.astype(jnp.bfloat16), jnp.concatenate(pieces, axis=1))


def solution(mesh):
    placed = (P("row", "col"), P(), P(), P("row", None))
    return jax.shard_map(
        body,
        mesh=mesh,
        in_specs=placed,
        out_specs=(P("row", "col"), P(("row", "col"), None)),
        check_vma=False,
    )
```

profile of v0, /device:TPU:0, one launch (start us, length us, event | category | flops | bytes accessed | tf_op | source)
XLA Modules:
  0.0 1086.1 jit_solution(1055814197106990699)
XLA Ops:
  32.2 11.7 %all-to-all-start = ((bf16[128,2,128,128]{3,2,1,0:T(8,128)(2,1)}), bf16[128,2,128,128]{3,2,1,0:T(8,128)(2,1)}, u32[]{:S(2)}, u32[]{:S(2)}) async-start(bf16[128,2,128,128]{3,2,1,0:T(8,128)(2,1)} %bitcast.164), calls=%async_computation | async-start | bytes 16777216 | tf_op jit(solution)/shard_map/all_to_all | solution.py:44
  54.0 88.6 %all-to-all-done = bf16[128,2,128,128]{3,2,1,0:T(8,128)(2,1)} async-done(((bf16[128,2,128,128]{3,2,1,0:T(8,128)(2,1)}), bf16[128,2,128,128]{3,2,1,0:T(8,128)(2,1)}, u32[]{:S(2)}, u32[]{:S(2)}) %all-to-all-start) | async-done | bytes 8388640 | tf_op jit(solution)/shard_map/all_to_all | solution.py:44
  142.6 11.2 %bitcast_convert_fusion = f32[256,128,128]{2,1,0:T(8,128)} fusion(bf16[128,2,128,128]{3,2,1,0:T(8,128)(2,1)} %all-to-all-done), kind=kLoop, calls=%fused_computation.14 | loop fusion | flops 4194304 | bytes 25165824 | tf_op jit(solution)/shard_map/reshape | solution.py:56
  158.2 56.8 %scatter_fusion = f32[129,128,128]{2,1,0:T(8,128)} fusion(f32[129,128,128]{2,1,0:T(8,128)} %broadcast_in_dim.76, s32[256]{0:T(256)S(1)} %reshape.285, f32[256,128,128]{2,1,0:T(8,128)} %bitcast_convert_fusion), kind=kCustom, calls=%fused_computation.2 | custom fusion | flops 4194304 | bytes 50332672 | tf_op jit(solution)/shard_map/scatter-add | solution.py:55
  235.2 10.4 bitcast_multiply_fusion.2
  251.6 106.9 %all-reduce.8.cloned.1.call-done = f32[2048,512]{0,1:T(8,128)} async-done(((f32[2048,512]{0,1:T(8,128)}), f32[2048,512]{0,1:T(8,128)}) %all-reduce.8.cloned.1.call-update) | async-done | bytes 4194320 | tf_op jit(solution)/shard_map/psum | solution.py:14
  361.1 62.6 %all-reduce.10.cloned.1.call-done = f32[512,512]{0,1:T(8,128)} async-done(((f32[512,512]{0,1:T(8,128)}), f32[512,512]{0,1:T(8,128)}) %all-reduce.10.cloned.1.call-update) | async-done | bytes 1048592 | tf_op jit(solution)/shard_map/psum | solution.py:14
  426.8 11.7 %cholesky.286 = f32[128,128]{1,0:T(8,128)S(1)} custom-call(f32[128,128]{1,0:T(8,128)S(1)} %cholesky.426), custom_call_target="Cholesky" | custom-call | tf_op jit(solution)/shard_map/jit(cholesky)/cholesky | solution.py:84
  449.2 11.7 %cholesky.305 = f32[128,128]{1,0:T(8,128)S(1)} custom-call(f32[128,128]{1,0:T(8,128)S(1)} %cholesky.430), custom_call_target="Cholesky" | custom-call | tf_op jit(solution)/shard_map/jit(cholesky)/cholesky | solution.py:84
  460.9 10.2 custom-call.30
  471.8 11.7 %cholesky.326 = f32[128,128]{1,0:T(8,128)S(1)} custom-call(f32[128,128]{1,0:T(8,128)S(1)} %cholesky.435), custom_call_target="Cholesky" | custom-call | tf_op jit(solution)/shard_map/jit(cholesky)/cholesky | solution.py:84
  494.6 11.7 %cholesky.343 = f32[128,128]{1,0:T(8,128)S(1)} custom-call(f32[128,128]{1,0:T(8,128)S(1)} %convolution_subtract_fusion.11), custom_call_target="Cholesky" | custom-call | tf_op jit(solution)/shard_map/jit(cholesky)/cholesky | solution.py:84
  518.6 39.3 %custom-call.32 = f32[4,128,128]{1,2,0:T(8,128)S(1)} custom-call(f32[4,128,128]{2,1,0:T(8,128)S(1)} %get-tuple-element.42), custom_call_target="InvertDiagBlocksLowerTriangular" | custom-call | tf_op jit(solution)/shard_map/triangular_solve/custom-call.3 | solution.py:85
  572.6 65.0 %all-reduce.12.cloned.1.call-done = f32[1024,512]{0,1:T(8,128)} async-done(((f32[1024,512]{0,1:T(8,128)}), f32[1024,512]{0,1:T(8,128)}) %all-reduce.12.cloned.1.call-update) | async-done | bytes 2097168 | tf_op jit(solution)/shard_map/psum | solution.py:14
  639.8 20.3 %fusion.2 = f32[2048,1024]{0,1:T(8,128)S(1)} fusion(f32[2048,1024]{0,1:T(8,128)} %copy-done.1, f32[128,8,16,128]{3,2,1,0:T(8,128)S(1)} %bitcast.162, f32[2048,512]{0,1:T(8,128)S(1)} %copy-done.3, f32[1024,512]{0,1:T(8,128)} %all-reduce.12.cloned.1.call-done), kind=kOutput, calls=%fused_computation.11 | convolution fusion | flops 12889096192 | bytes 31457280 | tf_op jit(solution)/shard_map/dot_general | solution.py:98
  665.6 102.8 %all-reduce.14.cloned.1.call-done = f32[2048,512]{0,1:T(8,128)} async-done(((f32[2048,512]{0,1:T(8,128)}), f32[2048,512]{0,1:T(8,128)}) %all-reduce.14.cloned.1.call-update) | async-done | bytes 4194320 | tf_op jit(solution)/shard_map/psum | solution.py:14
  771.2 62.1 %all-reduce.16.cloned.1.call-done = f32[512,512]{0,1:T(8,128)} async-done(((f32[512,512]{0,1:T(8,128)}), f32[512,512]{0,1:T(8,128)}) %all-reduce.16.cloned.1.call-update) | async-done | bytes 1048592 | tf_op jit(solution)/shard_map/psum | solution.py:14
  836.3 11.7 %cholesky.358 = f32[128,128]{1,0:T(8,128)S(1)} custom-call(f32[128,128]{1,0:T(8,128)S(1)} %cholesky.439), custom_call_target="Cholesky" | custom-call | tf_op jit(solution)/shard_map/jit(cholesky)/cholesky | solution.py:84
  858.7 11.7 %cholesky.377 = f32[128,128]{1,0:T(8,128)S(1)} custom-call(f32[128,128]{1,0:T(8,128)S(1)} %cholesky.443), custom_call_target="Cholesky" | custom-call | tf_op jit(solution)/shard_map/jit(cholesky)/cholesky | solution.py:84
  882.4 11.7 %cholesky.398 = f32[128,128]{1,0:T(8,128)S(1)} custom-call(f32[128,128]{1,0:T(8,128)S(1)} %cholesky.448), custom_call_target="Cholesky" | custom-call | tf_op jit(solution)/shard_map/jit(cholesky)/cholesky | solution.py:84
  905.3 11.7 %cholesky.415 = f32[128,128]{1,0:T(8,128)S(1)} custom-call(f32[128,128]{1,0:T(8,128)S(1)} %convolution_subtract_fusion.10), custom_call_target="Cholesky" | custom-call | tf_op jit(solution)/shard_map/jit(cholesky)/cholesky | solution.py:84
  928.9 39.3 %custom-call.36 = f32[4,128,128]{1,2,0:T(8,128)S(1)} custom-call(f32[4,128,128]{2,1,0:T(8,128)S(1)} %get-tuple-element.43), custom_call_target="InvertDiagBlocksLowerTriangular" | custom-call | tf_op jit(solution)/shard_map/triangular_solve/custom-call.3 | solution.py:85
  985.6 62.3 %all-reduce.18.cloned.1.call-done = f32[1024,512]{0,1:T(8,128)} async-done(((f32[1024,512]{0,1:T(8,128)}), f32[1024,512]{0,1:T(8,128)}) %all-reduce.18.cloned.1.call-update) | async-done | bytes 2097168 | tf_op jit(solution)/shard_map/psum | solution.py:14
  1050.7 21.7 %fusion.1 = bf16[2048,1024]{0,1:T(8,128)(2,1)} fusion(f32[2048,1024]{0,1:T(8,128)} %copy-done, f32[128,8,16,128]{3,2,1,0:T(8,128)S(1)} %bitcast.163, f32[2048,512]{0,1:T(8,128)S(1)} %copy-done.5, f32[1024,512]{0,1:T(8,128)S(1)} %copy-done.11), kind=kOutput, calls=%fused_computation.9 | convolution fusion | flops 12891193344 | bytes 27262976 | tf_op jit(solution)/shard_map/dot_general | solution.py:98
  (185 shorter events, 216.7 us)
Async XLA Ops:
  32.2 110.4 %all-to-all-start = ((bf16[128,2,128,128]{3,2,1,0:T(8,128)(2,1)}), bf16[128,2,128,128]{3,2,1,0:T(8,128)(2,1)}, u32[]{:S(2)}, u32[]{:S(2)}) async-start(bf16[128,2,128,128]{3,2,1,0:T(8,128)(2,1)} %bitcast.164), calls=%async_computation | async-start | bytes 16777216 | tf_op jit(solution)/shard_map/all_to_all | solution.py:44
  43.9 314.5 %all-reduce.8.cloned.1.call-start = ((), (), s32[]{:S(2)}) async-start(), calls=%async_computation.1 | async-start | bytes 8388608 | tf_op jit(solution)/shard_map/psum | solution.py:14
  231.9 3.4 copy-start.6
  245.7 3.2 copy-start.1
  251.5 172.3 %all-reduce.10.cloned.1.call-start = ((), (), s32[]{:S(2)}) async-start(), calls=%async_computation.2 | async-start | bytes 2097152 | tf_op jit(solution)/shard_map/psum | solution.py:14
  360.7 276.8 %all-reduce.12.cloned.1.call-start = ((), (), s32[]{:S(2)}) async-start(), calls=%async_computation.3 | async-start | bytes 4194304 | tf_op jit(solution)/shard_map/psum | solution.py:14
  361.1 198.9 %copy-start.9 = (f32[512,512]{1,0:T(8,128)}, f32[512,512]{1,0:T(8,128)S(1)}, u32[]{:S(2)}) copy-start(f32[512,512]{1,0:T(8,128)S(1)} %fusion.19) | copy-start | bytes 3145732
  557.9 3.2 copy-start.7
  568.7 2.0 copy-start.2
  572.2 196.2 %all-reduce.14.cloned.1.call-start = ((), (), s32[]{:S(2)}) async-start(), calls=%async_computation.4 | async-start | bytes 8388608 | tf_op jit(solution)/shard_map/psum | solution.py:14
  637.6 2.2 copy-start.3
  660.1 3.2 copy-start
  665.6 167.7 %all-reduce.16.cloned.1.call-start = ((), (), s32[]{:S(2)}) async-start(), calls=%async_computation.5 | async-start | bytes 2097152 | tf_op jit(solution)/shard_map/psum | solution.py:14
  770.8 277.1 %all-reduce.18.cloned.1.call-start = ((), (), s32[]{:S(2)}) async-start(), calls=%async_computation.6 | async-start | bytes 4194304 | tf_op jit(solution)/shard_map/psum | solution.py:14
  836.3 132.0 %copy-start.10 = (f32[512,512]{1,0:T(8,128)S(1)}, f32[512,512]{1,0:T(8,128)}, u32[]{:S(2)}) copy-start(f32[512,512]{1,0:T(8,128)} %copy-done.9) | copy-start | bytes 3145732
  968.3 3.2 copy-start.8
  979.1 2.0 copy-start.4
  1047.9 2.2 copy-start.5
  1047.9 2.9 copy-start.11
Sparse Core Ops, SparseCore 0:
  251.6 106.7 all-reduce.7
  361.4 62.3 all-reduce.9
  572.3 65.1 all-reduce.11
  665.7 102.7 all-reduce.13
  770.9 62.3 all-reduce.15
  982.7 65.1 all-reduce.17
where the time goes:
time: 1090 us
  waiting for transfers between devices  550 us (50%)
  other arithmetic  334 us (31%)
  local copies, waits for them, and re-layouts  95.7 us (9%)
  matrix products  72.4 us (7%)
  between operations  20.5 us (2%)
  starting transfers between devices  13.2 us (1%)
    psum x6, waiting for transfers between devices, broadcast(): return lax.psum(kept, axis)  462 us
    another operation x29, other arithmetic, body(): lower_factor = jnp.linalg.cholesky(diag_block)  158 us
    all_to_all x1, waiting for transfers between devices, body(): lax.all_to_all(outgoing, ('row', 'col'), split_axis=0, concat_axis=0, til...  88.6 us
    another operation x5, other arithmetic, body(): lax.linalg.triangular_solve(lower_factor, identity, left_side=True, lower...  79.1 us
    scatter-add x1, other arithmetic, body(): jax.ops.segment_sum(received.astype(jnp.float32).reshape(-1, tile_size, t...  56.8 us
    dot_general x2, matrix products, body(): jnp.dot(factor, across.T, precision=lax.Precision.HIGHEST, preferred_elem...  42 us
    unnamed x28, local copies, waits for them, and re-layouts  30.9 us
  transfers between devices with their start and end apart: 7, of which 7 were waited for; matrix products, arithmetic and copies ran while one was open for 1% of the time, Pallas kernels for 0%

commit v1 on v0

v1 whole, which is shorter than its diff:
```python
import jax
import jax.numpy as jnp
from jax import lax
from jax.experimental import pallas as pl
from jax.experimental.pallas import tpu as pltpu
from jax.sharding import Mesh, PartitionSpec as P

F32 = jnp.float32
BF16 = jnp.bfloat16
I32 = jnp.int32
T = 128
PW = 512
ROW = ("z", "core")
COL = ("y", "x")
ALL = ROW + COL
LOWER = [(i, j) for i in range(4) for j in range(i + 1)] + [
    (i, j) for i in range(4, 8) for j in range(i + 1)
]
HI = lax.Precision.HIGHEST
MIB = 2**20


def nt(a, b, precision=None):
    return lax.dot_general(
        a, b, (((1,), (1,)), ((), ())), precision=precision, preferred_element_type=F32
    )


def nn(a, b, precision=None):
    return lax.dot_general(
        a, b, (((1,), (0,)), ((), ())), precision=precision, preferred_element_type=F32
    )


def halves(x):
    high = x.astype(BF16)
    return high, (x - high.astype(F32)).astype(BF16)


def nt3(a_high, a_low, b_high, b_low):
    return nt(a_high, b_high) + (nt(a_high, b_low) + nt(a_low, b_high))


def lanes(x, j):
    return jnp.broadcast_to(x[:, j : j + 1], x.shape)


def subs(x, i):
    return jnp.broadcast_to(x[i : i + 1, :], x.shape)


def rsqrt(d):
    r = lax.rsqrt(d)
    return r * (1.5 - 0.5 * d * r * r)


def invert_block(load, store):
    rest = [load(s) for s in range(16)]
    sub = lax.broadcasted_iota(I32, (8, T), 0)
    lane = lax.broadcasted_iota(I32, (8, T), 1)
    right = [(lane == sub + 8 * s).astype(F32) for s in range(16)]
    for s in range(16):
        col = [lanes(rest[s], 8 * s + t) for t in range(8)]
        a = {(i, t): subs(col[t], i) for t in range(8) for i in range(t, 8)}
        rs = []
        for t in range(8):
            rs.append(rsqrt(a[t, t]))
            for i in range(t + 1, 8):
                a[i, t] = a[i, t] * rs[t]
            for m in range(t + 1, 8):
                for i in range(m, 8):
                    a[i, m] = a[i, m] - a[i, t] * a[m, t]
        u, w = [], []
        for t in range(8):
            x, y = subs(rest[s], t), subs(right[s], t)
            for m in range(t):
                x = x - a[t, m] * u[m]
                y = y - a[t, m] * w[m]
            u.append(x * rs[t])
            w.append(y * rs[t])
        out = w[0]
        for t in range(1, 8):
            out = jnp.where(sub == t, w[t], out)
        store(s, out)
        for n in range(s + 1, 16):
            c = []
            for t in range(8):
                x = lanes(rest[n], 8 * s + t)
                for m in range(t):
                    x = x - a[t, m] * c[m]
                c.append(x * rs[t])
            x, y = rest[n], right[n]
            for t in range(8):
                x = x - c[t] * u[t]
                y = y - c[t] * w[t]
            rest[n], right[n] = x, y


def panels_kernel(lead_ref, i1h, i1l, lh, ll, i2h, i2l, a, inv, i1, i2):
    for n, (i, j) in enumerate(LOWER):
        a[i * T : i * T + T, j * T : j * T + T] = lead_ref[n]
    i1[...] = jnp.zeros((PW, PW), F32)
    i2[...] = jnp.zeros((PW, PW), F32)

    def step(k, _):
        kk = pl.multiple_of(k * T, T)

        def load(s):
            return a[pl.ds(kk + 8 * s, 8), pl.ds(kk, T)]

        def store(s, v):
            inv[8 * s : 8 * s + 8, :] = v

        invert_block(load, store)
        for i in range(8):

            @pl.when(k == i)
            def _():
                p, b = divmod(i, 4)
                out = (i1, i2)[p]
                lo = T * b
                v = inv[...]
                if b:
                    out[lo : lo + T, :lo] = nn(v, out[lo : lo + T, :lo], HI)
                out[lo : lo + T, lo : lo + T] = v
                top = T * (i + 1)
                if top < 1024:
                    col = nt(a[top:, top - T : top], v, HI)
                    if p == 0:
                        lh[:, lo : lo + T], ll[:, lo : lo + T] = halves(col[PW - top :])
                    for j in range(i + 1, 8):
                        r = T * j
                        a[r:, r : r + T] -= nt(
                            col[r - top :], col[r - top : r - top + T], HI
                        )
                    if b < 3:
                        n = PW * (p + 1) - top
                        out[lo + T :, : lo + T] -= nn(col[:n], out[lo : lo + T, : lo + T], HI)

        return 0

    lax.fori_loop(0, 8, step, 0)
    i1h[...], i1l[...] = halves(i1[...])
    i2h[...], i2l[...] = halves(i2[...])


def panels(lead):
    s = jax.ShapeDtypeStruct((PW, PW), BF16)
    vmem = pl.BlockSpec(memory_space=pltpu.VMEM)
    return pl.pallas_call(
        panels_kernel,
        out_shape=(s,) * 6,
        in_specs=[vmem],
        out_specs=[vmem] * 6,
        scratch_shapes=[
            pltpu.VMEM((1024, 1024), F32),
            pltpu.VMEM((T, T), F32),
            pltpu.VMEM((PW, PW), F32),
            pltpu.VMEM((PW, PW), F32),
        ],
        compiler_params=pltpu.CompilerParams(vmem_limit_bytes=40 * MIB),
        cost_estimate=pl.CostEstimate(flops=20 * 10**9, bytes_accessed=8 * MIB, transcendentals=0),
        name="panels",
    )(lead)


def pack_kernel(tab, top, low, out):
    for t, ref in enumerate((top, low)):
        for q in range(16):
            k = pl.multiple_of(tab[16 + q] * T, T)
            out[q, t] = ref[:, pl.ds(k, T)]


def pack(children, tab):
    return pl.pallas_call(
        pack_kernel,
        out_shape=jax.ShapeDtypeStruct((128, 2, T, T), BF16),
        grid_spec=pltpu.PrefetchScalarGridSpec(
            num_scalar_prefetch=1,
            grid=(8,),
            in_specs=[
                pl.BlockSpec((T, PW), lambda p, tab: (tab[2 * p], 0)),
                pl.BlockSpec((T, PW), lambda p, tab: (tab[2 * p + 1], 0)),
            ],
            out_specs=pl.BlockSpec((16, 2, T, T), lambda p, tab: (p, 0, 0, 0)),
        ),
        compiler_params=pltpu.CompilerParams(vmem_limit_bytes=16 * MIB),
        cost_estimate=pl.CostEstimate(flops=0, bytes_accessed=10 * MIB, transcendentals=0),
        name="pack",
    )(tab, children, children)


def strip_kernel(tab, buf, own, out):
    i = pl.program_id(0)
    for j in range(8):
        part = own[:, j * T : j * T + T].astype(F32)
        kept = tab[48 + i * 8 + j] != 0
        for h in range(2):
            x = part[64 * h : 64 * h + 64]
            for c in range(2):
                rs, cs = tab[c * 16 + i], tab[32 + c * 8 + j]
                valid = jnp.logical_and(rs >= 0, cs >= 0)
                rs, cs = jnp.maximum(rs, 0), jnp.maximum(cs, 0)
                a, t = rs // 2, rs % 2
                y, slot = cs // 2, cs % 2
                n = (y * 4 + t * 2 + h) * 16 + (c * 4 + a) * 2 + slot
                x = x + jnp.where(valid, buf[n].astype(F32), 0.0)
            out[64 * h : 64 * h + 64, j * T : j * T + T] = jnp.where(kept, x, 0.0)


def strip_rows(tab, buf, own):
    return pl.pallas_call(
        strip_kernel,
        out_shape=jax.ShapeDtypeStruct((2048, 1024), F32),
        grid_spec=pltpu.PrefetchScalarGridSpec(
            num_scalar_prefetch=1,
            grid=(16,),
            in_specs=[
                pl.BlockSpec((256, 64, T), lambda i, tab: (0, 0, 0)),
                pl.BlockSpec((T, 1024), lambda i, tab: (i, 0)),
            ],
            out_specs=pl.BlockSpec((T, 1024), lambda i, tab: (i, 0)),
        ),
        compiler_params=pltpu.CompilerParams(vmem_limit_bytes=24 * MIB),
        cost_estimate=pl.CostEstimate(flops=10**7, bytes_accessed=16 * MIB, transcendentals=0),
        name="strip",
    )(tab, buf, own)


TM = 256
QS = 1024 // TM
RS = 2048 // TM


def update_kernel(tab, sq, sr, own, buf, i1h, i1l, lh, ll, i2h, i2l, out, fac, qh, ql):
    step = pl.program_id(0)

    def factor_rows(s, base, first):
        s0h, s0l = halves(s[:, :PW])
        f0 = nt3(s0h, s0l, i1h[...], i1l[...])
        f0h, f0l = halves(f0)
        up = nt3(f0h, f0l, lh[...], ll[...])
        rows = []
        for g in range(TM // T):
            cols = []
            for j in range(4):
                keep = jnp.logical_and(tab[base + g * 8 + 4 + j] != 0, first + g >= 4)
                piece = s[g * T : g * T + T, PW + j * T : PW + j * T + T]
                cols.append(
                    piece - jnp.where(keep, up[g * T : g * T + T, j * T : j * T + T], 0.0)
                )
            rows.append(jnp.concatenate(cols, axis=1))
        t1h, t1l = halves(jnp.concatenate(rows, axis=0))
        f1 = nt3(t1h, t1l, i2h[...], i2l[...])
        f1 = jnp.concatenate(
            [
                jnp.where(first + g >= 4, f1[g * T : g * T + T], 0.0)
                for g in range(TM // T)
            ],
            axis=0,
        )
        return f0, f1

    def operand(f0, f1, first):
        f0 = jnp.concatenate(
            [jnp.where(first + g >= 4, f0[g * T : g * T + T], 0.0) for g in range(TM // T)], axis=0
        )
        f1 = jnp.concatenate(
            [jnp.where(first + g >= 8, f1[g * T : g * T + T], 0.0) for g in range(TM // T)], axis=0
        )
        return halves(jnp.concatenate([f0, f1], axis=1))

    @pl.when(step < QS)
    def _():
        n = step * (TM // T)
        first = tab[369] + n
        f0, f1 = factor_rows(sq[...], 304 + n * 8, first)
        at = pl.ds(pl.multiple_of(step * TM, TM), TM)
        qh[at, :], ql[at, :] = operand(f0, f1, first)

    @pl.when(step >= QS)
    def _():
        n = (step - QS) * (TM // T)
        first = tab[368] + n
        f0, f1 = factor_rows(sr[...], 176 + n * 8, first)
        for g in range(TM // T):

            @pl.when(tab[371] == n + g)
            def _():
                fac[:, :PW] = f0[g * T : g * T + T]
                fac[:, PW:] = f1[g * T : g * T + T]

        fh, fl = operand(f0, f1, first)
        at_left = tab[371] == 0
        for h in range(4):
            qr = slice(h * 256, h * 256 + 256)
            up = nt3(fh, fl, qh[qr, :], ql[qr, :])
            for g in range(TM // T):
                for e in range(2):
                    j = h * 2 + e
                    x = jnp.where(
                        at_left, own[g * T : g * T + T, j * T : j * T + T].astype(F32), 0.0
                    )
                    for c in range(2):
                        rs, cs = tab[c * 16 + n + g], tab[32 + c * 8 + j]
                        valid = jnp.logical_and(rs >= 0, cs >= 0)
                        rs, cs = jnp.maximum(rs, 0), jnp.maximum(cs, 0)
                        a, t = rs // 2, rs % 2
                        src = ((c * 4 + a) * 16 + cs) * 2 + t
                        x = x + jnp.where(valid, buf[src].astype(F32), 0.0)
                    x = x - up[g * T : g * T + T, e * T : e * T + T]
                    kept = tab[48 + (n + g) * 8 + j] != 0
                    out[g * T : g * T + T, j * T : j * T + T] = jnp.where(kept, x, 0.0).astype(
                        BF16
                    )


def update(tab, sq, sr, own, buf, factors):
    small = pl.BlockSpec((PW, PW), lambda i, tab: (0, 0))

    def q_block(i, tab):
        j = jnp.minimum(i, QS - 1)
        half = QS // 2
        return ((j // half) ^ tab[370]) * half + j % half, 0

    def r_block(i, tab):
        return jnp.maximum(i - QS, 0), 0

    return pl.pallas_call(
        update_kernel,
        out_shape=(
            jax.ShapeDtypeStruct((2048, 1024), BF16),
            jax.ShapeDtypeStruct((T, 1024), F32),
        ),
        grid_spec=pltpu.PrefetchScalarGridSpec(
            num_scalar_prefetch=1,
            grid=(QS + RS,),
            in_specs=[
                pl.BlockSpec((TM, 1024), q_block),
                pl.BlockSpec((TM, 1024), r_block),
                pl.BlockSpec((TM, 1024), r_block),
                pl.BlockSpec((256, T, T), lambda i, tab: (0, 0, 0)),
            ]
            + [small] * 6,
            out_specs=[
                pl.BlockSpec((TM, 1024), r_block),
                pl.BlockSpec((T, 1024), lambda i, tab: (0, 0)),
            ],
            scratch_shapes=[pltpu.VMEM((1024, 1024), BF16), pltpu.VMEM((1024, 1024), BF16)],
        ),
        compiler_params=pltpu.CompilerParams(vmem_limit_bytes=56 * MIB),
        cost_estimate=pl.CostEstimate(
            flops=24 * 10**9, bytes_accessed=32 * MIB, transcendentals=0
        ),
        name="update",
    )(tab, sq, sr, own, buf, *factors)


def body(children, child_maps, pattern, own_cols):
    row = lax.axis_index(ROW)
    col = lax.axis_index(COL)
    core = lax.axis_index("core")
    child = row // 4
    pick = lambda x, n: lax.dynamic_index_in_dim(x, n, 0, keepdims=False)

    groups = child_maps.reshape(8, 16)
    home = groups // 16
    earlier = jnp.arange(16)[None, :] < jnp.arange(16)[:, None]
    rank = jnp.sum(((home[:, :, None] == home[:, None, :]) & earlier[None]).astype(I32), axis=2)
    slot = home * 2 + rank
    mine_slot = pick(slot, row)
    order = jnp.sum(
        jnp.where(mine_slot[None, :] == jnp.arange(16)[:, None], jnp.arange(16)[None, :], 0), axis=1
    )
    columns = child_maps.reshape(2, 16, 4)
    mine_columns = pick(pick(columns, child), col)
    source = jnp.sum(
        jnp.where(mine_columns[None, :] // 8 == jnp.arange(16)[:, None], jnp.arange(4)[None, :], 0),
        axis=1,
    )
    in_strip = jnp.any(columns < 8, axis=2)
    by_group = in_strip.reshape(2, 4, 4)
    before = jnp.arange(4)[None, :] < jnp.arange(4)[:, None]
    strip_rank = jnp.sum((by_group[:, :, None, :] & before[None, None]).astype(I32), axis=3)
    strip_place = (jnp.arange(4)[None, :, None] * 2 + strip_rank).reshape(2, 16)

    held = children.reshape(2048, 4, T)
    mine = lax.dynamic_slice(children, (0, source[0] * T), (2048, T)).reshape(16, T, T)[order]

    own_piece = lax.dynamic_slice(own_cols, (0, col * 64), (1024, 64))
    own_piece = own_piece.reshape(8, T, 64).transpose(1, 0, 2).reshape(T, 4, T)
    first = jnp.concatenate(
        [mine[:2].transpose(1, 0, 2), own_piece, jnp.zeros((T, 2, T), BF16)], axis=1
    )
    first = lax.all_to_all(first, ALL, 0, 0, tiled=True)
    lead_row = jnp.sum(
        jnp.where(slot[:, None, :] == jnp.arange(2)[None, :, None], groups[:, None, :] + 1, 0), axis=2
    ) - 1
    lead_row = jnp.where(lead_row < 8, lead_row, -1)
    lead_col = jnp.sum(jnp.where(columns < 8, columns + 1, 0), axis=2) - 1
    lead_col = jnp.repeat(lead_col, 4, axis=0)
    tile = jnp.where(
        (lead_row[:, None, :] >= 0) & (lead_col[:, :, None] >= 0),
        lead_row[:, None, :] * 8 + lead_col[:, :, None],
        -1,
    ).reshape(256)
    spread = (tile[None, :] == jnp.arange(64)[:, None]).astype(BF16)
    lead = nn(spread, first[:, :2].reshape(256, T))
    lead_own = first[:16, 2:6].reshape(16, 8, 64).transpose(1, 0, 2).reshape(64, T)
    lead = lead + lead_own.astype(F32)
    lead = jnp.stack([lead[i * 8 + j] for i, j in LOWER])
    lead = lax.all_to_all(jnp.broadcast_to(lead[None], (128, 36, T)), ALL, 0, 0, tiled=True)
    factors = panels(lead.transpose(1, 0, 2))

    strip = lax.all_to_all(mine.reshape(32, 64, T), ROW + ("x",), 0, 0, tiled=True)
    y = lax.axis_index("y")
    here = pick(by_group.transpose(1, 0, 2), y)
    here_rank = pick(strip_rank.transpose(1, 0, 2), y)
    from_x = jnp.sum(
        jnp.where(
            here[:, None, :] & (here_rank[:, None, :] == jnp.arange(2)[None, :, None]),
            jnp.arange(4)[None, None, :],
            0,
        ),
        axis=2,
    )
    strip = jnp.take_along_axis(
        strip.reshape(2, 4, 4, 64, T), from_x[:, None, :, None, None], axis=2
    )
    strip = lax.all_gather(strip, COL, axis=0, tiled=False).reshape(256, 64, T)

    my_tiles = row * 16 + jnp.arange(16)
    by_child = groups.reshape(2, 64)
    by_rank = (jnp.arange(4)[None, :, None] * 2 + rank.reshape(2, 4, 16)).reshape(2, 64)
    row_source = jnp.sum(
        jnp.where(by_child[:, None, :] == my_tiles[None, :, None], by_rank[:, None, :] + 1, 0), axis=2
    ) - 1
    flat = columns.reshape(2, 64)
    strip_source = jnp.sum(
        jnp.where(
            flat[:, None, :] == jnp.arange(8)[None, :, None],
            jnp.repeat(strip_place, 4, axis=1)[:, None, :] + 1,
            0,
        ),
        axis=2,
    ) - 1
    col_source = jnp.sum(
        jnp.where(
            flat[:, None, :] == (col * 8 + jnp.arange(8))[None, :, None],
            (jnp.arange(64) // 4 + 1)[None, None, :],
            0,
        ),
        axis=2,
    ) - 1
    pat_rows = lax.dynamic_slice(pattern, (row * 16, 0), (16, 128))
    pat_strip = pat_rows[:, :8].reshape(-1)
    pat_block = lax.dynamic_slice(pat_rows, (0, col * 8), (16, 8)).reshape(-1)
    pat_other = lax.dynamic_slice(pattern, (col * 8, 0), (8, 8)).reshape(-1)
    rows_flat = row_source.reshape(-1)
    strip = strip_rows(
        jnp.concatenate([rows_flat, strip_source.reshape(-1), pat_strip]).astype(I32), strip, own_cols
    )

    pairs = [
        (p * 16 + q, (q % 8) * 16 + 2 * p + q // 8) for p in range(8) for q in range(16)
    ]
    other = lax.dynamic_slice(strip, ((col // 8) * 1024 + (col % 2) * 512, 0), (512, 1024))
    other = lax.ppermute(other, ALL, pairs)
    swapped = lax.ppermute(other, "core", [(0, 1), (1, 0)])
    other = jnp.concatenate([other, swapped], axis=0)

    packed = pack(children, jnp.concatenate([order, source]).astype(I32))
    tiles = lax.all_to_all(packed, ALL, 0, 0, tiled=True).reshape(256, T, T)

    tab = jnp.concatenate(
        [
            rows_flat,
            col_source.reshape(-1),
            pat_block,
            pat_strip,
            pat_other,
            jnp.stack([row * 16, col * 8, core, col]),
        ]
    ).astype(I32)
    return update(tab, other, strip, own_cols, tiles, factors)


def solution(mesh):
    grid = Mesh(mesh.devices.reshape(4, 2, 4, 4), ALL)
    return jax.shard_map(
        body,
        mesh=grid,
        in_specs=(P(ROW, COL), P(), P(), P(ROW, None)),
        out_specs=(P(ROW, COL), P(ALL, None)),
        check_vma=False,
    )
```

time: 1090 us -> 512 us (0.47)
  the two profiles are of different devices: /device:TPU:0 before, /device:TPU:47 now
where the time goes in v1:
time: 512 us; the launch traced here: 511 us
  waiting for transfers between devices  318 us (62%)
  Pallas kernels  102 us (20%)
  starting transfers between devices  38 us (7%)
  local copies, waits for them, and re-layouts  32.5 us (6%)
  between operations  14.5 us (3%)
  other arithmetic  6.31 us (1%)
    ppermute x1, waiting for transfers between devices, body(): other = lax.ppermute(other, ALL, pairs)  181 us
    all_gather x1, waiting for transfers between devices, body(): strip = lax.all_gather(strip, COL, axis=0, tiled=False).reshape(256, 64, T)  98.8 us
    pallas_call x1, Pallas kernels, panels(): pl.pallas_call(panels_kernel, out_shape=(s,) * 6, in_specs=[vmem], out_sp...  51.4 us
    pallas_call x1, Pallas kernels, update(): pl.pallas_call(update_kernel, out_shape=(jax.ShapeDtypeStruct((2048, 1024...  43.2 us
    all_to_all x1, waiting for transfers between devices, body(): lax.all_to_all(jnp.broadcast_to(lead[None], (128, 36, T)), ALL, 0, 0, til...  27.8 us
    unnamed x25, local copies, waits for them, and re-layouts  15.6 us
  transfers between devices with their start and end apart: 7, of which 5 were waited for; matrix products, arithmetic and copies ran while one was open for 4% of the time, Pallas kernels for 11%

profile of v1, /device:TPU:47, one launch (start us, length us, event | category | flops | bytes accessed | tf_op | source)
XLA Modules:
  0.0 511.2 jit_solution(7760927993585953343)
XLA Ops:
  9.4 1.1 constant_dynamic-slice_fusion.3
  10.4 1.4 gather_fusion
  11.8 8.3 %all-to-all-start = ((bf16[32,64,128]{2,1,0:T(8,128)(2,1)}), bf16[32,64,128]{2,1,0:T(8,128)(2,1)S(1)}, u32[]{:S(2)}, u32[]{:S(2)}) async-start(bf16[32,64,128]{2,1,0:T(8,128)(2,1)} %bitcast.11), calls=%async_computation | async-start | bytes 1048576 | tf_op jit(solution)/shard_map/all_to_all | solution.py:415
  21.6 1.1 constant_dynamic-slice_fusion
  24.1 5.1 all-to-all-done
  29.2 8.8 %all-to-all-start.2 = ((bf16[128,8,128]{2,1,0:T(8,128)(2,1)}), bf16[128,8,128]{2,1,0:T(8,128)(2,1)S(1)}, u32[]{:S(2)}, u32[]{:S(2)}) async-start(bf16[128,8,128]{2,1,0:T(8,128)(2,1)} %copy.35), calls=%async_computation.2 | async-start | bytes 524288 | tf_op jit(solution)/shard_map/all_to_all | solution.py:395
  40.3 5.1 all-to-all-done.2
  46.2 1.7 broadcast_in_dim.163
  47.9 9.2 %all-to-all-start.3 = ((f32[128,36,128]{2,1,0:T(8,128)}), f32[128,36,128]{2,1,0:T(8,128)}, u32[]{:S(2)}, u32[]{:S(2)}) async-start(f32[128,36,128]{2,1,0:T(8,128)} %broadcast_in_dim.163), calls=%async_computation.3 | async-start | bytes 5242880 | tf_op jit(solution)/shard_map/all_to_all | solution.py:412
  57.2 2.3 pack.1
  59.5 3.2 copy-done
  62.7 27.8 %all-to-all-done.3 = f32[128,36,128]{2,1,0:T(8,128)} async-done(((f32[128,36,128]{2,1,0:T(8,128)}), f32[128,36,128]{2,1,0:T(8,128)}, u32[]{:S(2)}, u32[]{:S(2)}) %all-to-all-start.3) | async-done | bytes 2359328 | tf_op jit(solution)/shard_map/all_to_all | solution.py:412
  90.5 9.7 %all-to-all-start.1 = ((bf16[128,2,128,128]{3,2,1,0:T(8,128)(2,1)}), bf16[128,2,128,128]{3,2,1,0:T(8,128)(2,1)}, u32[]{:S(2)}, u32[]{:S(2)}) async-start(bf16[128,2,128,128]{3,2,1,0:T(8,128)(2,1)} %copy-done), calls=%async_computation.1 | async-start | bytes 16777216 | tf_op jit(solution)/shard_map/all_to_all | solution.py:473
  102.6 98.8 %all-gather.2.cloned.1.call-done = bf16[16,2,4,2,64,128]{5,4,3,2,1,0:T(8,128)(2,1)} async-done(((bf16[1,2,4,2,64,128]{5,4,3,2,1,0:T(8,128)(2,1)}), bf16[16,2,4,2,64,128]{5,4,3,2,1,0:T(8,128)(2,1)}) %all-gather.2.cloned.1.call-update) | async-done | bytes 4194320 | tf_op jit(solution)/shard_map/all_gather | solution.py:430
  201.3 2.2 copy-done.3
  203.5 2.2 copy-done.4
  205.7 5.0 strip.1.sr
  210.8 3.2 copy-done.1
  214.1 1.9 collective-permute-start
  216.0 181.0 %collective-permute-done = f32[512,1024]{1,0:T(8,128)S(1)} collective-permute-done((f32[512,1024]{1,0:T(8,128)S(1)}, f32[512,1024]{1,0:T(8,128)S(1)}, u32[]{:S(2)}, u32[]{:S(2)}) %collective-permute-start) | collective-permute-done | bytes 2097184 | tf_op jit(solution)/shard_map/ppermute | solution.py:468
  398.6 2.2 copy.43
  400.8 51.4 %panels.1 = (bf16[512,512]{1,0:T(8,128)(2,1)S(1)}, bf16[512,512]{1,0:T(8,128)(2,1)S(1)}, bf16[512,512]{1,0:T(8,128)(2,1)S(1)}, bf16[512,512]{1,0:T(8,128)(2,1)S(...) custom-call(f32[36,128,128]{2,1,0:T(8,128)S(1)} %bitcast.49), custom_call_target="tpu_custom_call" | custom-call | flops 20000000000 | bytes 8388608 | tf_op jit(solution)/shard_map/panels/pallas_call | solution.py:150
  457.0 4.1 pad_maximum_fusion.sq
  461.1 43.2 %update.1 = (bf16[2048,1024]{1,0:T(8,128)(2,1)}, f32[128,1024]{1,0:T(8,128)}) custom-call(s32[372]{0:T(512)} %concatenate.15.tab, f32[1024,1024]{1,0:T(8,128)} %pad_maximum_fusion.sq, f32[2048,1024]{1,0:T(8,128)} %copy-done.1, bf16[2048,1024]{1,0:T(8,128)(2,1)} %own.3, bf16[256,128,128]{2,1,0:T(8,128)(2,1)} %bitcast.18.buf, bf16[512,512]{1,0:T(8,128)(2,1)} %copy-done.5, ...), custom_call_target="tpu_custom_call" | custom-call | flops 24000000000 | bytes 33554432 | tf_op jit(solution)/shard_map/update/pallas_call | solution.py:329
  (114 shorter events, 16.7 us)
Async XLA Ops:
  11.8 17.4 %all-to-all-start = ((bf16[32,64,128]{2,1,0:T(8,128)(2,1)}), bf16[32,64,128]{2,1,0:T(8,128)(2,1)S(1)}, u32[]{:S(2)}, u32[]{:S(2)}) async-start(bf16[32,64,128]{2,1,0:T(8,128)(2,1)} %bitcast.11), calls=%async_computation | async-start | bytes 1048576 | tf_op jit(solution)/shard_map/all_to_all | solution.py:415
  29.2 16.2 %all-to-all-start.2 = ((bf16[128,8,128]{2,1,0:T(8,128)(2,1)}), bf16[128,8,128]{2,1,0:T(8,128)(2,1)S(1)}, u32[]{:S(2)}, u32[]{:S(2)}) async-start(bf16[128,8,128]{2,1,0:T(8,128)(2,1)} %copy.35), calls=%async_computation.2 | async-start | bytes 524288 | tf_op jit(solution)/shard_map/all_to_all | solution.py:395
  38.0 163.3 %all-gather.2.cloned.1.call-start = ((), (), s32[]{:S(2)}) async-start(), calls=%async_computation.4 | async-start | bytes 4456448 | tf_op jit(solution)/shard_map/all_gather | solution.py:430
  45.5 11.7 %copy-start.2 = (bf16[2048,512]{1,0:T(8,128)(2,1)S(1)}, bf16[2048,512]{1,0:T(8,128)(2,1)}, u32[]{:S(2)}) copy-start(bf16[2048,512]{1,0:T(8,128)(2,1)} %low.1) | copy-start | bytes 6291460
  47.9 42.6 %all-to-all-start.3 = ((f32[128,36,128]{2,1,0:T(8,128)}), f32[128,36,128]{2,1,0:T(8,128)}, u32[]{:S(2)}, u32[]{:S(2)}) async-start(f32[128,36,128]{2,1,0:T(8,128)} %broadcast_in_dim.163), calls=%async_computation.3 | async-start | bytes 5242880 | tf_op jit(solution)/shard_map/all_to_all | solution.py:412
  59.5 3.2 copy-start
  62.7 37.9 %copy-start.11 = (s32[2,64]{1,0:T(2,128)S(1)}, s32[2,64]{1,0:T(2,128)}, u32[]{:S(2)}) copy-start(s32[2,64]{1,0:T(2,128)} %param.5) | copy-start | bytes 1540
  90.5 370.6 %all-to-all-start.1 = ((bf16[128,2,128,128]{3,2,1,0:T(8,128)(2,1)}), bf16[128,2,128,128]{3,2,1,0:T(8,128)(2,1)}, u32[]{:S(2)}, u32[]{:S(2)}) async-start(bf16[128,2,128,128]{3,2,1,0:T(8,128)(2,1)} %copy-done), calls=%async_computation.1 | async-start | bytes 16777216 | tf_op jit(solution)/shard_map/all_to_all | solution.py:473
  201.3 2.2 copy-start.3
  203.5 2.2 copy-start.4
  210.7 3.2 copy-start.1
  214.1 182.9 %collective-permute-start = (f32[512,1024]{1,0:T(8,128)S(1)}, f32[512,1024]{1,0:T(8,128)S(1)}, u32[]{:S(2)}, u32[]{:S(2)}) collective-permute-start(f32[512,1024]{1,0:T(8,128)S(1)} %constant_dynamic-slice_fusion.1), channel_id=1, source_target_pairs={{0,0},{1,16},{2,32},{3,48},{4,64},{5,80},{6,96},{7,112},{8,1},{9,1... | collective-permute-start | bytes 6291464 | tf_op jit(solution)/shard_map/ppermute | solution.py:468
  397.0 60.0 %collective-permute-start.1 = (f32[512,1024]{1,0:T(8,128)S(1)}, f32[512,1024]{1,0:T(8,128)}, u32[]{:S(2)}, u32[]{:S(2)}) collective-permute-start(f32[512,1024]{1,0:T(8,128)S(1)} %collective-permute-done), channel_id=1, source_target_pairs={{0,16},{16,0},{1,17},{17,1},{2,18},{18,2},{3,19},{19,3},{4,20},{20... | collective-permute-start | bytes 6291464 | tf_op jit(solution)/shard_map/ppermute | solution.py:469
  452.2 0.8 copy-start.5
  453.0 0.8 copy-start.6
  453.8 0.8 copy-start.7
  454.6 0.8 copy-start.8
  455.4 0.8 copy-start.9
  456.2 0.8 copy-start.10
Sparse Core Ops, SparseCore 0:
  41.6 159.6 all-gather.1
